TPU v7x, 32 devices: a whole 2x2x4 slice. The times are simulated.
32 devices in a mesh: rows: 4 (over y, core), cols: 8 (over z, x).
Axes of the slice: x: 2, y: 2, z: 4, core: 2. Of those that a mesh axis runs over, the one named last changes fastest.
Arguments:
- iterate: bfloat16 [3584, 20480], P('rows', 'cols'), may hold values from -4.5 to 4.5
Outputs:
- updated: bfloat16 [3584, 20480], P('rows', 'cols')
All inputs are finite; a program needn't handle non-finite values.
Results may differ from a plain program's by a relative error of at most 0.0054.
Values may be sent and summed in bfloat16 or wider, within the bound.
A program may use at most 128 MiB of HBM per device.

v0:
```python
import jax
import jax.numpy as jnp
from jax import lax
from jax.sharding import PartitionSpec as P

linear_coef = 3.4445
cubic_coef = -4.775
quintic_coef = 2.0315


def shifted(value, axis, steps):
    count = lax.axis_size(axis)
    pairs = [(source, (source + steps) % count) for source in range(count)]
    return lax.ppermute(value, axis, pairs)


def dot_rows(left, right):
    return lax.dot_general(
        left, right, (((1,), (1,)), ((), ())), preferred_element_type=jnp.float32
    )


def on_device(iterate):
    row_count = lax.axis_size("rows")
    row_index = lax.axis_index("rows")
    col_index = lax.axis_index("cols")
    row_block = iterate.shape[0]
    col_width = iterate.shape[1]
    half_cols = col_width // 2
    vocab_total = col_width * lax.axis_size("cols")
    full_rows = row_block * row_count
    slab_width = full_rows // lax.axis_size("cols")
    own_half = row_index // 2
    mine_half = lax.dynamic_slice_in_dim(iterate, own_half * half_cols, half_cols, 1)
    all_rows = lax.all_gather(iterate, "rows", axis=0, tiled=True)
    next_block = lax.dynamic_slice_in_dim(
        all_rows, (row_index + 1) % row_count * row_block, row_block, 0
    )
    across = lax.dynamic_slice(
        all_rows,
        ((row_index + 2) % row_count * row_block, own_half * half_cols),
        (row_block, half_cols),
    )
    diag_tile = dot_rows(iterate, iterate)
    upper_tile = dot_rows(iterate, next_block)
    far_part = dot_rows(mine_half, across)
    shares = (
        lax.psum_scatter(diag_tile, "cols", scatter_dimension=0, tiled=True),
        lax.psum_scatter(upper_tile, "cols", scatter_dimension=0, tiled=True),
        lax.psum_scatter(far_part, "cols", scatter_dimension=0, tiled=True),
    )
    diag_share = (shares[0] / vocab_total).astype(jnp.bfloat16)
    upper_share = (shares[1] / vocab_total).astype(jnp.bfloat16)
    diag_gram, upper_gram = (
        lax.all_gather(diag_share, "cols", axis=0, tiled=True),
        lax.all_gather(upper_share, "cols", axis=0, tiled=True),
    )
    far_sum = lax.all_gather(
        (shares[2] / vocab_total).astype(jnp.bfloat16), "cols", axis=0, tiled=True
    ).astype(jnp.float32)
    left_tile = shifted(upper_gram, "rows", 1)
    far_other = shifted(far_sum.astype(jnp.bfloat16), "rows", 2).astype(far_sum.dtype)
    far_gram = (far_sum + far_other.T).astype(jnp.bfloat16)
    rolled = jnp.concatenate([diag_gram, upper_gram, far_gram, left_tile.T], axis=1)
    doubled = jnp.concatenate([rolled, rolled], axis=1)
    gram_rows = lax.dynamic_slice_in_dim(
        doubled, (row_count - row_index) % row_count * row_block, full_rows, 1
    )
    gram_slab = lax.dynamic_slice_in_dim(gram_rows, col_index * slab_width, slab_width, 1)
    gram_column = lax.all_gather(gram_slab, "rows", axis=0, tiled=True)
    square = jnp.dot(gram_rows, gram_column, preferred_element_type=jnp.float32)
    poly_slab = (cubic_coef * gram_slab.astype(jnp.float32) + quintic_coef * square).astype(
        jnp.bfloat16
    )
    poly_rows = lax.all_gather(poly_slab, "cols", axis=1, tiled=True)
    linear_part = linear_coef * iterate.astype(jnp.float32)
    mixed = linear_part + jnp.dot(poly_rows, all_rows, preferred_element_type=jnp.float32)
    return mixed.astype(jnp.bfloat16)


def solution(mesh):
    return jax.shard_map(
        on_device,
        mesh=mesh,
        in_specs=(P("rows", "cols"),),
        out_specs=P("rows", "cols"),
        check_vma=False,
    )
```

profile of v0, /device:TPU:0, one launch (start us, length us, event | category | flops | bytes accessed | tf_op | source)
XLA Modules:
  0.0 693.6 jit_solution(15453572276359156252)
XLA Ops:
  6.5 0.0 all-gather.9.cloned.1.call-start
  6.5 0.7 all-gather.9.cloned.1.call-update
  7.3 0.0 reduce-scatter.12.cloned.1.call-start
  7.3 121.4 %all-gather.9.cloned.1.call-done = bf16[3584,2560]{1,0:T(8,128)(2,1)} async-done(((bf16[896,2560]{1,0:T(8,128)(2,1)}), bf16[3584,2560]{1,0:T(8,128)(2,1)}) %all-gather.9.cloned.1.call-update) | async-done | bytes 18350096 | tf_op jit(solution)/shard_map/all_gather | solution.py:35
  128.8 6.6 fusion.5
  135.3 0.0 reduce-scatter.12.cloned.1.call-update
  135.4 0.0 reduce-scatter.10.cloned.1.call-start
  135.4 8.1 %fusion.8 = f32[896,896]{0,1:T(8,128)S(1)} fusion(bf16[896,2560]{1,0:T(8,128)(2,1)} %param.1, bf16[3584,2560]{1,0:T(8,128)(2,1)} %all-gather.9.cloned.1.call-done, s32[]{:T(128)S(6)} %select_n.40), kind=kOutput, calls=%fused_computation.10 | convolution fusion | flops 4110417920 | bytes 12386308 | tf_op jit(solution)/shard_map/dot_general | solution.py:18
  143.6 3.0 copy.14
  146.6 0.0 reduce-scatter.10.cloned.1.call-update
  146.6 0.0 reduce-scatter.8.cloned.1.call-start
  146.7 10.4 %fusion.18 = f32[896,896]{1,0:T(8,128)} fusion(bf16[896,2560]{1,0:T(8,128)(2,1)} %param.1), kind=kOutput, calls=%fused_computation.27 | convolution fusion | flops 4110417920 | bytes 7798784 | tf_op jit(solution)/shard_map/dot_general | solution.py:18
  157.0 0.0 reduce-scatter.8.cloned.1.call-update
  157.1 0.0 all-gather.13.cloned.1.call-start
  157.1 54.3 %reduce-scatter.12.cloned.1.call-done = f32[112,896]{1,0:T(8,128)} async-done(((f32[896,896]{1,0:T(8,128)}), f32[112,896]{1,0:T(8,128)}) %reduce-scatter.12.cloned.1.call-update) | async-done | bytes 401424 | tf_op jit(solution)/shard_map/reduce_scatter | solution.py:50
  211.4 1.7 multiply_convert_fusion
  213.1 0.0 all-gather.13.cloned.1.call-update
  213.1 0.0 all-gather.11.cloned.1.call-start
  213.2 77.4 %reduce-scatter.10.cloned.1.call-done = f32[112,896]{1,0:T(8,128)} async-done(((f32[896,896]{1,0:T(8,128)}), f32[112,896]{1,0:T(8,128)}) %reduce-scatter.10.cloned.1.call-update) | async-done | bytes 401424 | tf_op jit(solution)/shard_map/reduce_scatter | solution.py:49
  290.5 1.7 multiply_convert_fusion.1
  292.3 0.0 all-gather.11.cloned.1.call-update
  292.3 0.0 all-gather.7.cloned.1.call-start
  292.3 76.8 %reduce-scatter.8.cloned.1.call-done = f32[112,896]{1,0:T(8,128)} async-done(((f32[896,896]{1,0:T(8,128)}), f32[112,896]{1,0:T(8,128)}) %reduce-scatter.8.cloned.1.call-update) | async-done | bytes 401424 | tf_op jit(solution)/shard_map/reduce_scatter | solution.py:48
  369.2 1.7 multiply_convert_fusion.2
  370.9 0.0 all-gather.7.cloned.1.call-update
  370.9 0.0 all-gather.15.cloned.1.call-start
  371.0 43.7 %all-gather.13.cloned.1.call-done = bf16[896,896]{1,0:T(8,128)(2,1)} async-done(((bf16[112,896]{1,0:T(8,128)(2,1)}), bf16[896,896]{1,0:T(8,128)(2,1)}) %all-gather.13.cloned.1.call-update) | async-done | bytes 1605648 | tf_op jit(solution)/shard_map/all_gather | solution.py:58
  414.7 3.6 copy.10
  418.3 0.0 copy-start
  418.3 1.5 collective-permute-start
  419.7 40.6 %all-gather.11.cloned.1.call-done = bf16[896,896]{1,0:T(8,128)(2,1)} async-done(((bf16[112,896]{1,0:T(8,128)(2,1)}), bf16[896,896]{1,0:T(8,128)(2,1)}) %all-gather.11.cloned.1.call-update) | async-done | bytes 1605648 | tf_op jit(solution)/shard_map/all_gather | solution.py:56
  460.3 0.0 copy-start.1
  460.3 3.7 copy.11
  464.0 0.0 collective-permute-start.1
  464.0 42.1 %all-gather.7.cloned.1.call-done = bf16[896,896]{1,0:T(8,128)(2,1)} async-done(((bf16[112,896]{1,0:T(8,128)(2,1)}), bf16[896,896]{1,0:T(8,128)(2,1)}) %all-gather.7.cloned.1.call-update) | async-done | bytes 1605648 | tf_op jit(solution)/shard_map/all_gather | solution.py:55
  506.1 1.7 constant_dynamic-update-slice_fusion.3
  507.8 0.0 copy-done.1
  507.8 0.3 constant_dynamic-update-slice_fusion.2
  508.1 0.0 copy-start.2
  508.1 0.0 collective-permute-done
  508.1 0.0 copy-done
  508.1 2.0 fusion.13
  510.1 0.0 collective-permute-done.1
  510.1 1.7 bitcast_dynamic-update-slice_fusion
  511.8 0.0 copy-done.2
  511.9 0.3 constant_dynamic-update-slice_fusion.1
  512.1 0.3 constant_dynamic-update-slice_fusion
  512.4 1.9 fusion.14
  514.4 1.7 bitcast_dynamic-update-slice_fusion.1
  516.1 0.0 copy-start.3
  516.1 4.6 copy-done.3
  520.7 1.4 constant_dynamic-slice_fusion
  522.1 0.0 all-gather.15.cloned.1.call-update
  522.1 0.2 all-gather.17.cloned.1.call-start
  522.3 30.2 %all-gather.15.cloned.1.call-done = bf16[3584,448]{1,0:T(8,128)(2,1)} async-done(((bf16[896,448]{1,0:T(8,128)(2,1)}), bf16[3584,448]{1,0:T(8,128)(2,1)}) %all-gather.15.cloned.1.call-update) | async-done | bytes 3211280 | tf_op jit(solution)/shard_map/all_gather | solution.py:70
  552.6 7.6 %add_convert_fusion.1 = bf16[896,448]{1,0:T(8,128)(2,1)S(1)} fusion(bf16[896,448]{1,0:T(8,128)(2,1)} %constant_dynamic-slice_fusion, bf16[3584,448]{1,0:T(8,128)(2,1)} %all-gather.15.cloned.1.call-done, bf16[896,7168]{1,0:T(8,128)(2,1)} %copy-done.3, s32[]{:T(128)S(6)} %select_n.48), kind=kOutput, calls=%fused_computation.11 | convolution fusion | flops 2879299584 | bytes 11812868 | tf_op jit(solution)/shard_map/dot_general | solution.py:71
  560.2 1.2 copy.12
  561.4 0.0 all-gather.17.cloned.1.call-update
  561.5 100.8 %all-gather.17.cloned.1.call-done = bf16[896,3584]{0,1:T(8,128)(2,1)} async-done(((bf16[896,448]{0,1:T(8,128)(2,1)}), bf16[896,3584]{0,1:T(8,128)(2,1)}) %all-gather.17.cloned.1.call-update) | async-done | bytes 6422544 | tf_op jit(solution)/shard_map/all_gather | solution.py:75
  662.2 24.8 %add_convert_fusion = bf16[896,2560]{1,0:T(8,128)(2,1)} fusion(bf16[896,2560]{1,0:T(8,128)(2,1)} %param.1, bf16[896,3584]{0,1:T(8,128)(2,1)} %all-gather.17.cloned.1.call-done, bf16[3584,2560]{1,0:T(8,128)(2,1)} %all-gather.9.cloned.1.call-done), kind=kOutput, calls=%fused_computation | convolution fusion | flops 16450846720 | bytes 33947648 | tf_op jit(solution)/shard_map/dot_general | solution.py:77
Async XLA Ops:
  6.5 122.2 %all-gather.9.cloned.1.call-start = ((), (), s32[]{:S(2)}) async-start(), calls=%async_computation.5 | async-start | bytes 22937600 | tf_op jit(solution)/shard_map/all_gather | solution.py:35
  7.3 204.1 %reduce-scatter.12.cloned.1.call-start = ((), (), s32[]{:S(2)}) async-start(), calls=%async_computation.11 | async-start | bytes 3612672 | tf_op jit(solution)/shard_map/reduce_scatter | solution.py:50
  135.4 155.2 %reduce-scatter.10.cloned.1.call-start = ((), (), s32[]{:S(2)}) async-start(), calls=%async_computation.10 | async-start | bytes 3612672 | tf_op jit(solution)/shard_map/reduce_scatter | solution.py:49
  146.6 222.5 %reduce-scatter.8.cloned.1.call-start = ((), (), s32[]{:S(2)}) async-start(), calls=%async_computation.3 | async-start | bytes 3612672 | tf_op jit(solution)/shard_map/reduce_scatter | solution.py:48
  157.1 257.6 %all-gather.13.cloned.1.call-start = ((), (), s32[]{:S(2)}) async-start(), calls=%async_computation.7 | async-start | bytes 1806336 | tf_op jit(solution)/shard_map/all_gather | solution.py:58
  213.1 247.2 %all-gather.11.cloned.1.call-start = ((), (), s32[]{:S(2)}) async-start(), calls=%async_computation.6 | async-start | bytes 1806336 | tf_op jit(solution)/shard_map/all_gather | solution.py:56
  292.3 213.8 %all-gather.7.cloned.1.call-start = ((), (), s32[]{:S(2)}) async-start(), calls=%async_computation.4 | async-start | bytes 1806336 | tf_op jit(solution)/shard_map/all_gather | solution.py:55
  370.9 181.7 %all-gather.15.cloned.1.call-start = ((), (), s32[]{:S(2)}) async-start(), calls=%async_computation.8 | async-start | bytes 4587520 | tf_op jit(solution)/shard_map/all_gather | solution.py:70
  418.3 89.8 %copy-start = (bf16[896,896]{1,0:T(8,128)(2,1)S(1)}, bf16[896,896]{1,0:T(8,128)(2,1)}, u32[]{:S(2)}) copy-start(bf16[896,896]{1,0:T(8,128)(2,1)} %all-gather.13.cloned.1.call-done) | copy-start | bytes 4816900
  418.3 89.8 %collective-permute-start = (bf16[896,896]{0,1:T(8,128)(2,1)}, bf16[896,896]{0,1:T(8,128)(2,1)}, u32[]{:S(2)}, u32[]{:S(2)}) collective-permute-start(bf16[896,896]{0,1:T(8,128)(2,1)} %copy.10), channel_id=1, source_target_pairs={{0,16},{8,24},{16,0},{24,8},{1,17},{9,25},{17,1},{25,9},{2,18},{10... | collective-permute-start | bytes 4816904 | tf_op jit(solution)/shard_map/ppermute | solution.py:14
  460.3 47.4 %copy-start.1 = (bf16[896,896]{1,0:T(8,128)(2,1)S(1)}, bf16[896,896]{1,0:T(8,128)(2,1)}, u32[]{:S(2)}) copy-start(bf16[896,896]{1,0:T(8,128)(2,1)} %all-gather.11.cloned.1.call-done) | copy-start | bytes 4816900
  464.0 46.1 %collective-permute-start.1 = (bf16[896,896]{0,1:T(8,128)(2,1)}, bf16[896,896]{0,1:T(8,128)(2,1)}, u32[]{:S(2)}, u32[]{:S(2)}) collective-permute-start(bf16[896,896]{0,1:T(8,128)(2,1)} %copy.11), channel_id=1, source_target_pairs={{0,8},{8,16},{16,24},{24,0},{1,9},{9,17},{17,25},{25,1},{2,10},{10... | collective-permute-start | bytes 4816904 | tf_op jit(solution)/shard_map/ppermute | solution.py:14
  508.1 3.8 copy-start.2
  516.1 4.6 copy-start.3
  522.1 140.1 %all-gather.17.cloned.1.call-start = ((), (), s32[]{:S(2)}) async-start(), calls=%async_computation.9 | async-start | bytes 7225344 | tf_op jit(solution)/shard_map/all_gather | solution.py:75
Sparse Core Ops, SparseCore 0:
  8.9 119.8 all-gather.8
  135.5 75.8 reduce-scatter.11
  215.4 75.0 reduce-scatter.9
  294.0 75.1 reduce-scatter.7
  371.4 43.2 all-gather.12
  416.9 43.3 all-gather.10
  462.7 43.3 all-gather.6
  522.2 30.3 all-gather.14
  561.6 100.6 all-gather.16
where the time goes:
time: 694 us
  waiting for transfers between devices  588 us (85%)
  matrix products  57.5 us (8%)
  local copies, waits for them, and re-layouts  23.4 us (3%)
  between operations  13.4 us (2%)
  other arithmetic  9.11 us (1%)
    all_gather x1, waiting for transfers between devices, on_device(): all_rows = lax.all_gather(iterate, 'rows', axis=0, tiled=True)  121 us
    all_gather x1, waiting for transfers between devices, on_device(): poly_rows = lax.all_gather(poly_slab, 'cols', axis=1, tiled=True)  101 us
    reduce_scatter x1, waiting for transfers between devices, on_device(): lax.psum_scatter(upper_tile, 'cols', scatter_dimension=0, tiled=True)  77.4 us
    reduce_scatter x1, waiting for transfers between devices, on_device(): lax.psum_scatter(diag_tile, 'cols', scatter_dimension=0, tiled=True)  76.8 us
    reduce_scatter x1, waiting for transfers between devices, on_device(): lax.psum_scatter(far_part, 'cols', scatter_dimension=0, tiled=True)  54.3 us
    all_gather x1, waiting for transfers between devices, on_device(): lax.all_gather((shares[2] / vocab_total).astype(jnp.bfloat16), 'cols', ax...  43.7 us
    all_gather x1, waiting for transfers between devices, on_device(): lax.all_gather(diag_share, 'cols', axis=0, tiled=True)  42.1 us
    all_gather x1, waiting for transfers between devices, on_device(): lax.all_gather(upper_share, 'cols', axis=0, tiled=True)  40.6 us
  transfers between devices with their start and end apart: 11, of which 9 were waited for; matrix products, arithmetic and copies ran while one was open for 5% of the time, Pallas kernels for 0%

commit v1 on v0

v1 whole, which is shorter than its diff:
```python
import functools

import jax
import jax.numpy as jnp
from jax import lax
from jax.experimental import pallas as pl
from jax.experimental.pallas import tpu as pltpu
from jax.sharding import PartitionSpec as P

linear_coef = 3.4445
cubic_coef = -4.775
quintic_coef = 2.0315

MESH = pl.DeviceIdType.MESH
ANY = pl.BlockSpec(memory_space=pl.ANY)
bf16 = jnp.bfloat16


def greet(peers):
    barrier = pltpu.get_barrier_semaphore()
    for peer in peers:
        pl.semaphore_signal(barrier, inc=1, device_id=peer, device_id_type=MESH)
    pl.semaphore_wait(barrier, len(peers))


def remote(src, dst, send, recv, peer):
    return pltpu.make_async_remote_copy(
        src_ref=src, dst_ref=dst, send_sem=send, recv_sem=recv, device_id=peer, device_id_type=MESH
    )


def flip(index, bit):
    return index + bit - 2 * bit * ((index // bit) % 2)


def place():
    row, col = lax.axis_index("rows"), lax.axis_index("cols")
    return row, col


def pair_kernel(chunks, x_ref, pair_ref, send, recv, local):
    row, col = place()
    sibling = (flip(row, 1), col)
    core = row % 2
    greet([sibling])
    size = x_ref.shape[0] // chunks
    copies = []
    for j in range(chunks):
        part = pl.ds(j * size, size)
        copy = remote(x_ref.at[part], pair_ref.at[core, part], send.at[j], recv.at[j], sibling)
        copy.start()
        copies.append(copy)
    own = pltpu.make_async_copy(x_ref, pair_ref.at[core], local)
    own.start()
    for copy in copies:
        copy.wait()
    own.wait()


def start_scatter(cols, part_ref, got_ref, send, recv, local):
    row, col = place()
    copies = []
    for k in range(1, cols):
        dest = (col + k) % cols
        copy = remote(part_ref.at[dest], got_ref.at[k], send.at[k], recv.at[k], (row, dest))
        copy.start()
        copies.append(copy)
    own = pltpu.make_async_copy(part_ref.at[col], got_ref.at[0], local)
    own.start()
    copies.append(own)
    return copies


def rows_kernel(
    cols, chunks, pair_ref, part_ref, all_ref, got_ref,
    y_send, y_recv, f_send, f_recv, s_send, s_recv, local,
):
    row, col = place()
    core = row % 2
    across, sibling = (flip(row, 2), col), (flip(row, 1), col)
    greet([across, sibling] + [(row, (col + k) % cols) for k in range(1, cols)])
    size = pair_ref.shape[1] // chunks
    parts = [pl.ds(j * size, size) for j in range(chunks)]
    outgoing = []
    for j, part in enumerate(parts):
        copy = remote(
            pair_ref.at[core, part], all_ref.at[row, part], y_send.at[j], y_recv.at[j], across
        )
        copy.start()
        outgoing.append(copy)
    scatter = start_scatter(cols, part_ref, got_ref, s_send, s_recv, local.at[0])
    keep = pltpu.make_async_copy(pair_ref, all_ref.at[pl.ds(row - core, 2)], local.at[1])
    keep.start()
    forwards = []
    for j, part in enumerate(parts):
        outgoing[j].wait_recv()
        there = all_ref.at[flip(row, 2), part]
        copy = remote(there, there, f_send.at[j], f_recv.at[j], sibling)
        copy.start()
        forwards.append(copy)
    for copy in outgoing:
        copy.wait_send()
    for copy in scatter + [keep] + forwards:
        copy.wait()


def gather(rows, cols, share_ref, all_ref, send, recv, local):
    row, col = place()
    side, across, sibling = (row, flip(col, 1)), (flip(row, 2), col), (flip(row, 1), col)
    group = cols // 2
    sent = []

    def push(src, r, c, peer):
        copy = remote(src, all_ref.at[r, c], send.at[len(sent)], recv.at[r, c], peer)
        copy.start()
        sent.append(copy)

    def arrived(r, c):
        slot = all_ref.at[r, c]
        remote(slot, slot, send.at[0], recv.at[r, c], sibling).wait_recv()

    def member(m):
        return ((col // 2 + m) % group) * 2 + col % 2

    for m in range(1, group):
        push(share_ref, row, col, (row, member(group - m)))
    push(share_ref, row, col, side)
    push(share_ref, row, col, across)
    push(share_ref, row, col, sibling)
    own = pltpu.make_async_copy(share_ref, all_ref.at[row, col], local)
    own.start()
    far = flip(row, 2)
    for m in range(1, group):
        c = member(m)
        arrived(row, c)
        for peer in (side, across, sibling):
            push(all_ref.at[row, c], row, c, peer)
    for m in range(group):
        c = flip(member(m), 1)
        arrived(row, c)
        if 2 * m < group:
            push(all_ref.at[row, c], row, c, across)
        push(all_ref.at[row, c], row, c, sibling)
        c = member(m)
        arrived(far, c)
        if 2 * m >= group:
            push(all_ref.at[far, c], far, c, side)
        push(all_ref.at[far, c], far, c, sibling)
    for m in range(group):
        c = flip(member(m), 1)
        arrived(far, c)
        push(all_ref.at[far, c], far, c, sibling)
    for r in (flip(row, 1), flip(flip(row, 1), 2)):
        for c in range(cols):
            arrived(r, c)
    for copy in sent:
        copy.wait_send()
    own.wait()


def gather_sends(cols):
    group = cols // 2
    return (group - 1) + 3 + 3 * (group - 1) + 3 * group + group


def gather_peers(cols):
    row, col = place()
    return [(flip(row, 2), col), (flip(row, 1), col)] + [(row, (col + k) % cols) for k in range(1, cols)]


def both_kernel(rows, cols, part_ref, share_ref, got_ref, all_ref, s_send, s_recv, g_send, g_recv, local):
    greet(gather_peers(cols))
    scatter = start_scatter(cols, part_ref, got_ref, s_send, s_recv, local.at[0])
    gather(rows, cols, share_ref, all_ref, g_send, g_recv, local.at[1])
    for copy in scatter:
        copy.wait()


def gather_kernel(rows, cols, share_ref, all_ref, g_send, g_recv, local):
    greet(gather_peers(cols))
    gather(rows, cols, share_ref, all_ref, g_send, g_recv, local.at[0])


def call(kernel, ident, args, outs, sems):
    return pl.pallas_call(
        kernel,
        out_shape=outs,
        in_specs=[ANY] * len(args),
        out_specs=[ANY] * len(outs),
        scratch_shapes=[pltpu.SemaphoreType.DMA(shape) for shape in sems],
        compiler_params=pltpu.CompilerParams(collective_id=ident, has_side_effects=True),
    )(*args)


def dot_rows(left, right):
    return lax.dot_general(
        left, right, (((1,), (1,)), ((), ())), preferred_element_type=jnp.float32
    )


def round_up(value, unit):
    return -(-value // unit) * unit


def chunked(tile, cols):
    count = round_up(-(-tile.shape[0] // cols), 16)
    tile = jnp.pad(tile, ((0, count * cols - tile.shape[0]), (0, 0)))
    return tile.reshape(cols, count, tile.shape[1])


def on_device(iterate):
    rows, cols = lax.axis_size("rows"), lax.axis_size("cols")
    row = lax.axis_index("rows")
    block, width = iterate.shape
    half = block // 2
    vocab = width * cols
    full = block * rows
    chunks = 8

    def shape(*dims):
        return jax.ShapeDtypeStruct(dims, bf16)

    (pair,) = call(
        functools.partial(pair_kernel, 4), 1, [iterate], [shape(2, block, width)], [(4,), (4,), ()]
    )
    top = lax.dynamic_slice(pair, (0, (row % 2) * half, 0), (1, half, width))[0]
    near = jnp.concatenate(
        [dot_rows(iterate, iterate).astype(bf16), dot_rows(top, pair[1]).astype(bf16)], axis=0
    )
    near = chunked(near, cols)
    near_rows = near.shape[1]
    all_rows, got = call(
        functools.partial(rows_kernel, cols, chunks),
        2,
        [pair, near],
        [shape(rows, block, width), shape(cols, near_rows, block)],
        [(chunks,)] * 4 + [(cols,), (cols,), (2,)],
    )

    def summed(parts):
        return (jnp.sum(parts.astype(jnp.float32), axis=0) / vocab).astype(bf16)

    near_share = summed(got)
    other = jnp.where(row < 2, row + 2, rows - 1 - row)
    cross = dot_rows(iterate, lax.dynamic_index_in_dim(all_rows, other, 0, keepdims=False)).astype(bf16)
    cross = chunked(cross, cols)
    cross_rows = cross.shape[1]
    sends = gather_sends(cols)
    got, near_all = call(
        functools.partial(both_kernel, rows, cols),
        3,
        [cross, near_share],
        [shape(cols, cross_rows, block), shape(rows, cols, near_rows, block)],
        [(cols,), (cols,), (sends,), (rows, cols), (2,)],
    )
    (cross_all,) = call(
        functools.partial(gather_kernel, rows, cols),
        4,
        [summed(got)],
        [shape(rows, cols, cross_rows, block)],
        [(sends,), (rows, cols), (2,)],
    )
    near_all = near_all.reshape(rows, cols * near_rows, block)
    cross_all = cross_all.reshape(rows, cols * cross_rows, block)[:, :block]
    diag = near_all[:, :block]
    ab = near_all[0:2, block : block + half].reshape(block, block)
    cd = near_all[2:4, block : block + half].reshape(block, block)
    ac, bd, cb, da = cross_all[0], cross_all[1], cross_all[2], cross_all[3]
    gram = jnp.concatenate(
        [
            jnp.concatenate([diag[0], ab, ac, da.T], axis=1),
            jnp.concatenate([ab.T, diag[1], cb.T, bd], axis=1),
            jnp.concatenate([ac.T, cb, diag[2], cd], axis=1),
            jnp.concatenate([da, bd.T, cd.T, diag[3]], axis=1),
        ],
        axis=0,
    )
    gram_rows = lax.dynamic_slice_in_dim(gram, row * block, block, 0)
    square = jnp.dot(gram_rows, gram, preferred_element_type=jnp.float32)
    poly = (cubic_coef * gram_rows.astype(jnp.float32) + quintic_coef * square).astype(bf16)
    linear_part = linear_coef * iterate.astype(jnp.float32)
    mixed = linear_part + jnp.dot(
        poly, all_rows.reshape(full, width), preferred_element_type=jnp.float32
    )
    return mixed.astype(bf16)


def solution(mesh):
    return jax.shard_map(
        on_device,
        mesh=mesh,
        in_specs=(P("rows", "cols"),),
        out_specs=P("rows", "cols"),
        check_vma=False,
    )
```

time: 694 us -> 783 us (1.13)
  waiting for transfers between devices: 588 us -> 0 us
  Pallas kernels: 0 us -> 577 us
  other arithmetic: 9.11 us -> 79 us
  local copies, waits for them, and re-layouts: 23.4 us -> 46.9 us
  matrix products: 57.5 us -> 79.1 us
  between operations: 13.4 us -> 0.1 us
    pallas_call x0 -> x4, Pallas kernels: none -> 577 us  [call(): pl.pallas_call(kernel, out_shape=outs, in_specs=[ANY] * len(args), out_sp...]
    all_gather x6 -> x0, waiting for transfers between devices: 379 us -> none  [the longest x1 121 us: on_device(): all_rows = lax.all_gather(iterate, 'rows', axis=0, tiled=True)]
    reduce_scatter x3 -> x0, waiting for transfers between devices: 208 us -> none  [the longest x1 77.4 us: on_device(): lax.psum_scatter(upper_tile, 'cols', scatter_dimension=0, tiled=True)]
    concatenate x0 -> x3, other arithmetic: none -> 73.7 us  [the longest x1 67 us: on_device(): jnp.concatenate([jnp.concatenate([diag[0], ab, ac, da.T], axis=1), jnp.co...]
    dot_general x2, matrix products: 32.4 us -> 55.1 us  [the longest x1 32.5 us: on_device(): square = jnp.dot(gram_rows, gram, preferred_element_type=jnp.float32)]
    squeeze x0 -> x5, local copies, waits for them, and re-layouts: none -> 20.6 us  [the longest x3 10.7 us: on_device(): ac, bd, cb, da = (cross_all[0], cross_all[1], cross_all[2], cross_all[3])]
    concatenate x1, local copies, waits for them, and re-layouts: 1.69 us -> 9.54 us  [on_device(): jnp.concatenate([diag[0], ab, ac, da.T], axis=1)]
    dot_general x2 -> x3, matrix products: 18.5 us -> 24 us  [dot_rows(): lax.dot_general(left, right, (((1,), (1,)), ((), ())), preferred_element_...]
  transfers between devices with their start and end apart: 11 -> 0, of which waited for: 9 -> 0; matrix products, arithmetic and copies ran while one was open for 5% -> 0% of each run, Pallas kernels for 0% -> 0%
where the time goes in v1:
time: 783 us; the launch traced here: 782 us
  Pallas kernels  577 us (74%)
  matrix products  79.1 us (10%)
  other arithmetic  79 us (10%)
  local copies, waits for them, and re-layouts  46.9 us (6%)
    pallas_call x4, Pallas kernels, call(): pl.pallas_call(kernel, out_shape=outs, in_specs=[ANY] * len(args), out_sp...  577 us
    concatenate x1, other arithmetic, on_device(): jnp.concatenate([jnp.concatenate([diag[0], ab, ac, da.T], axis=1), jnp.co...  67 us
    dot_general x1, matrix products, on_device(): square = jnp.dot(gram_rows, gram, preferred_element_type=jnp.float32)  32.5 us
    dot_general x3, matrix products, dot_rows(): lax.dot_general(left, right, (((1,), (1,)), ((), ())), preferred_element_...  24 us
    dot_general x1, matrix products, on_device(): jnp.dot(poly, all_rows.reshape(full, width), preferred_element_type=jnp.f...  22.6 us

profile of v1, /device:TPU:0, one launch (start us, length us, event | category | flops | bytes accessed | tf_op | source)
XLA Modules:
  0.0 781.7 jit_solution(7778147975114975836)
XLA Ops:
  0.0 8.6 %convolution_convert_fusion = bf16[896,896]{1,0:T(8,128)(2,1)S(1)} fusion(bf16[896,2560]{1,0:T(8,128)(2,1)} %x_ref.1), kind=kOutput, calls=%fused_computation.20 | convolution fusion | flops 4111220736 | bytes 6193152 | tf_op jit(solution)/shard_map/dot_general | solution.py:196
  8.6 140.6 %shard_map.17.pair_ref = bf16[2,896,2560]{2,1,0:T(8,128)(2,1)} custom-call(bf16[896,2560]{1,0:T(8,128)(2,1)} %x_ref.1), custom_call_target="tpu_custom_call" | custom-call | tf_op jit(solution)/shard_map/pallas_call | solution.py:185
  149.3 5.6 fusion.15
  154.8 1.7 fusion.9
  156.5 294.6 %shard_map.18 = (bf16[4,896,2560]{2,1,0:T(8,128)(2,1)}, bf16[8,176,896]{2,1,0:T(8,128)(2,1)}) custom-call(bf16[2,896,2560]{2,1,0:T(8,128)(2,1)} %shard_map.17.pair_ref, bf16[8,176,896]{2,1,0:T(8,128)(2,1)} %bitcast.61), custom_call_target="tpu_custom_call" | custom-call | tf_op jit(solution)/shard_map/pallas_call | solution.py:185
  451.1 2.1 convert_reduce_fusion
  453.3 0.8 multiply_convert_fusion.share_ref
  454.0 9.8 %fusion.12 = bf16[896,896]{0,1:T(8,128)(2,1)} fusion(bf16[896,2560]{1,0:T(8,128)(2,1)} %x_ref.1, bf16[4,896,2560]{2,1,0:T(8,128)(2,1)} %get-tuple-element.9, s32[]{:T(128)S(6)} %select_n.23), kind=kOutput, calls=%fused_computation.19 | convolution fusion | flops 4111220736 | bytes 10780676 | tf_op jit(solution)/shard_map/dot_general | solution.py:196
  463.8 98.0 %shard_map.19 = (bf16[8,112,896]{2,1,0:T(8,128)(2,1)}, bf16[4,8,176,896]{3,2,1,0:T(8,128)(2,1)}) custom-call(bf16[8,112,896]{2,1,0:T(8,128)(2,1)} %bitcast.69, bf16[176,896]{1,0:T(8,128)(2,1)} %multiply_convert_fusion.share_ref), custom_call_target="tpu_custom_call" | custom-call | tf_op jit(solution)/shard_map/pallas_call | solution.py:185
  561.8 1.7 convert_reduce_fusion.1
  563.4 0.7 multiply_convert_fusion.1.share_ref
  564.2 2.2 fusion.23
  566.3 0.0 copy-start
  566.3 6.3 slice_bitcast_fusion.1
  572.6 3.6 copy.21
  576.2 3.6 copy.19
  579.8 3.6 copy.22
  583.3 0.0 copy-done
  583.3 2.3 copy.17
  585.6 43.5 %shard_map.20 = bf16[4,8,112,896]{3,2,1,0:T(8,128)(2,1)} custom-call(bf16[112,896]{1,0:T(8,128)(2,1)} %multiply_convert_fusion.1.share_ref), custom_call_target="tpu_custom_call" | custom-call | tf_op jit(solution)/shard_map/pallas_call | solution.py:185
  629.1 5.1 fusion.24
  634.2 3.6 copy.12
  637.8 3.6 copy.16
  641.4 3.6 copy.14
  645.0 5.0 pad_maximum_fusion
  650.0 9.5 %copy.20 = bf16[896,3584]{0,1:T(8,128)(2,1)} copy(bf16[896,3584]{1,0:T(8,128)(2,1)} %pad_maximum_fusion) | data formatting | bytes 12845056 | tf_op jit(solution)/shard_map/concatenate | solution.py:271
  659.5 0.0 slice-start
  659.5 67.0 %maximum_maximum_fusion = bf16[3584,3584]{0,1:T(8,128)(2,1)} fusion(bf16[896,896]{0,1:T(8,128)(2,1)} %copy.19, bf16[896,896]{0,1:T(8,128)(2,1)} %bitcast.60, bf16[896,896]{0,1:T(8,128)(2,1)} %bitcast.55, bf16[896,896]{0,1:T(8,128)(2,1)} %copy.12, bf16[896,896]{0,1:T(8,128)(2,1)} %copy.17, bf16[896,896]{0,1:T(8,128)(2,1)} %bitcast.65, ...), kind=kLoop, calls=%fused_computation | loop fusion | flops 333971456 | bytes 51380224 | tf_op jit(solution)/shard_map/concatenate | solution.py:269
  726.6 0.0 slice-start.1
  726.6 32.5 %add_convert_fusion = bf16[896,3584]{0,1:T(8,128)(2,1)S(1)} fusion(bf16[3584,3584]{0,1:T(8,128)(2,1)} %maximum_maximum_fusion, s32[]{:T(128)S(6)} %select_n.24), kind=kOutput, calls=%fused_computation.1 | convolution fusion | flops 23034396672 | bytes 44958720 | tf_op jit(solution)/shard_map/dot_general | solution.py:279
  759.0 0.0 slice-done
  759.1 0.0 slice-done.1
  759.1 22.6 %add_convert_fusion.1 = bf16[896,2560]{1,0:T(8,128)(2,1)} fusion(bf16[896,2560]{1,0:T(8,128)(2,1)S(1)} %bitcast.68, bf16[896,3584]{0,1:T(8,128)(2,1)S(1)} %add_convert_fusion, bf16[3584,2560]{1,0:T(8,128)(2,1)} %bitcast.70), kind=kOutput, calls=%fused_computation.2 | convolution fusion | flops 16450846720 | bytes 33947648 | tf_op jit(solution)/shard_map/dot_general | solution.py:282
  (1 shorter events, 0.0 us)
Async XLA Ops:
  566.3 17.0 %copy-start = (bf16[2,448,896]{2,1,0:T(8,128)(2,1)}, bf16[2,448,896]{2,1,0:T(8,128)(2,1)S(1)}, u32[]{:S(2)}) copy-start(bf16[2,448,896]{2,1,0:T(8,128)(2,1)S(1)} %get-tuple-element.18) | copy-start | bytes 4816900
  659.5 99.5 %slice-start = ((s8[4587520]{0:T(1024)(128)(4,1)}), s8[4194304]{0:T(1024)(128)(4,1)S(1)}, s32[]{:S(2)}) async-start(s8[4587520]{0:T(1024)(128)(4,1)} %bitcast.67), calls=%async_computation | async-start | bytes 8388608
  726.6 32.5 %slice-start.1 = ((s8[4587520]{0:T(1024)(128)(4,1)}), s8[393216]{0:T(1024)(128)(4,1)S(1)}, s32[]{:S(2)}) async-start(s8[4587520]{0:T(1024)(128)(4,1)} %bitcast.67), calls=%async_computation.1 | async-start | bytes 786432

commit v2 on v1

--- a/solution.py
+++ b/solution.py
@@ -38,7 +38,14 @@
     return row, col
 
 
-def pair_kernel(chunks, x_ref, pair_ref, send, recv, local):
+def through_vmem(src, dst, held, sem):
+    for a, b in ((src, held), (held, dst)):
+        copy = pltpu.make_async_copy(a, b, sem)
+        copy.start()
+        copy.wait()
+
+
+def pair_kernel(chunks, x_ref, pair_ref, send, recv, local, held):
     row, col = place()
     sibling = (flip(row, 1), col)
     core = row % 2
@@ -50,14 +57,12 @@
         copy = remote(x_ref.at[part], pair_ref.at[core, part], send.at[j], recv.at[j], sibling)
         copy.start()
         copies.append(copy)
-    own = pltpu.make_async_copy(x_ref, pair_ref.at[core], local)
-    own.start()
+    through_vmem(x_ref, pair_ref.at[core], held, local)
     for copy in copies:
         copy.wait()
-    own.wait()
-
-
-def start_scatter(cols, part_ref, got_ref, send, recv, local):
+
+
+def start_scatter(cols, part_ref, got_ref, send, recv):
     row, col = place()
     copies = []
     for k in range(1, cols):
@@ -65,15 +70,12 @@
         copy = remote(part_ref.at[dest], got_ref.at[k], send.at[k], recv.at[k], (row, dest))
         copy.start()
         copies.append(copy)
-    own = pltpu.make_async_copy(part_ref.at[col], got_ref.at[0], local)
-    own.start()
-    copies.append(own)
     return copies
 
 
 def rows_kernel(
     cols, chunks, pair_ref, part_ref, all_ref, got_ref,
-    y_send, y_recv, f_send, f_recv, s_send, s_recv, local,
+    y_send, y_recv, f_send, f_recv, s_send, s_recv, local, held, small,
 ):
     row, col = place()
     core = row % 2
@@ -88,9 +90,9 @@
         )
         copy.start()
         outgoing.append(copy)
-    scatter = start_scatter(cols, part_ref, got_ref, s_send, s_recv, local.at[0])
-    keep = pltpu.make_async_copy(pair_ref, all_ref.at[pl.ds(row - core, 2)], local.at[1])
-    keep.start()
+    scatter = start_scatter(cols, part_ref, got_ref, s_send, s_recv)
+    through_vmem(part_ref.at[col], got_ref.at[0], small, local)
+    through_vmem(pair_ref, all_ref.at[pl.ds(row - core, 2)], held, local)
     forwards = []
     for j, part in enumerate(parts):
         outgoing[j].wait_recv()
@@ -100,11 +102,11 @@
         forwards.append(copy)
     for copy in outgoing:
         copy.wait_send()
-    for copy in scatter + [keep] + forwards:
+    for copy in scatter + forwards:
         copy.wait()
 
 
-def gather(rows, cols, share_ref, all_ref, send, recv, local):
+def gather(rows, cols, share_ref, all_ref, send, recv, local, held):
     row, col = place()
     side, across, sibling = (row, flip(col, 1)), (flip(row, 2), col), (flip(row, 1), col)
     group = cols // 2
@@ -127,8 +129,7 @@
     push(share_ref, row, col, side)
     push(share_ref, row, col, across)
     push(share_ref, row, col, sibling)
-    own = pltpu.make_async_copy(share_ref, all_ref.at[row, col], local)
-    own.start()
+    through_vmem(share_ref, all_ref.at[row, col], held, local)
     far = flip(row, 2)
     for m in range(1, group):
         c = member(m)
@@ -155,7 +156,6 @@
             arrived(r, c)
     for copy in sent:
         copy.wait_send()
-    own.wait()
 
 
 def gather_sends(cols):
@@ -168,27 +168,82 @@
     return [(flip(row, 2), col), (flip(row, 1), col)] + [(row, (col + k) % cols) for k in range(1, cols)]
 
 
-def both_kernel(rows, cols, part_ref, share_ref, got_ref, all_ref, s_send, s_recv, g_send, g_recv, local):
+def both_kernel(rows, cols, part_ref, share_ref, got_ref, all_ref, s_send, s_recv, g_send, g_recv, local, small, held):
     greet(gather_peers(cols))
-    scatter = start_scatter(cols, part_ref, got_ref, s_send, s_recv, local.at[0])
-    gather(rows, cols, share_ref, all_ref, g_send, g_recv, local.at[1])
+    scatter = start_scatter(cols, part_ref, got_ref, s_send, s_recv)
+    through_vmem(part_ref.at[lax.axis_index("cols")], got_ref.at[0], small, local)
+    gather(rows, cols, share_ref, all_ref, g_send, g_recv, local, held)
     for copy in scatter:
         copy.wait()
 
 
-def gather_kernel(rows, cols, share_ref, all_ref, g_send, g_recv, local):
+def gather_kernel(rows, cols, share_ref, all_ref, g_send, g_recv, local, held):
     greet(gather_peers(cols))
-    gather(rows, cols, share_ref, all_ref, g_send, g_recv, local.at[0])
-
-
-def call(kernel, ident, args, outs, sems):
+    gather(rows, cols, share_ref, all_ref, g_send, g_recv, local, held)
+
+
+def poly_kernel(near_ref, cross_ref, poly_ref, gram_ref):
+    block, tile = poly_ref.shape
+    half, strip = block // 2, 128
+    row, step = lax.axis_index("rows"), pl.program_id(0)
+
+    @pl.when(step == 0)
+    def _():
+        def put(i, j, start, source):
+            count = source.shape[0]
+            gram_ref[pl.ds(i * block + start, count), pl.ds(j * block, block)] = source[...]
+            if i != j:
+
+                @pl.loop(0, block, step=strip)
+                def _(at):
+                    gram_ref[
+                        pl.ds(pl.multiple_of(j * block + at, strip), strip), pl.ds(i * block + start, count)
+                    ] = source[:, pl.ds(pl.multiple_of(at, strip), strip)].T
+
+        for i in range(4):
+            put(i, i, 0, near_ref.at[i, pl.ds(0, block)])
+        for core in range(2):
+            put(0, 1, core * half, near_ref.at[core, pl.ds(block, half)])
+            put(2, 3, core * half, near_ref.at[2 + core, pl.ds(block, half)])
+        for r, (i, j) in enumerate(((0, 2), (1, 3), (2, 1), (3, 0))):
+            put(i, j, 0, cross_ref.at[r, pl.ds(0, block)])
+
+    mine = pl.ds(pl.multiple_of(row * block, block), block)
+    slab = pl.ds(pl.multiple_of(step * tile, tile), tile)
+    square = jnp.dot(gram_ref[mine, :], gram_ref[:, slab], preferred_element_type=jnp.float32)
+    gram = gram_ref[mine, slab].astype(jnp.float32)
+    poly_ref[...] = (cubic_coef * gram + quintic_coef * square).astype(bf16)
+
+
+def poly_rows(near, cross, block):
+    rows = near.shape[0]
+    full, tile = rows * block, 512
+
+    def whole(array):
+        return pl.BlockSpec(array.shape, lambda step: (0, 0, 0), pipeline_mode=pl.Buffered(1))
+
+    return pl.pallas_call(
+        poly_kernel,
+        grid=(full // tile,),
+        out_shape=jax.ShapeDtypeStruct((block, full), bf16),
+        in_specs=[whole(near), whole(cross)],
+        out_specs=pl.BlockSpec((block, tile), lambda step: (0, step)),
+        scratch_shapes=[pltpu.VMEM((full, full), bf16)],
+        compiler_params=pltpu.CompilerParams(vmem_limit_bytes=58 * 2**20),
+    )(near, cross)
+
+
+def call(kernel, ident, args, outs, sems, holds):
     return pl.pallas_call(
         kernel,
         out_shape=outs,
         in_specs=[ANY] * len(args),
         out_specs=[ANY] * len(outs),
-        scratch_shapes=[pltpu.SemaphoreType.DMA(shape) for shape in sems],
-        compiler_params=pltpu.CompilerParams(collective_id=ident, has_side_effects=True),
+        scratch_shapes=[pltpu.SemaphoreType.DMA(shape) for shape in sems]
+        + [pltpu.VMEM(shape, bf16) for shape in holds],
+        compiler_params=pltpu.CompilerParams(
+            collective_id=ident, has_side_effects=True, vmem_limit_bytes=32 * 2**20
+        ),
     )(*args)
 
 
@@ -221,7 +276,8 @@
         return jax.ShapeDtypeStruct(dims, bf16)
 
     (pair,) = call(
-        functools.partial(pair_kernel, 4), 1, [iterate], [shape(2, block, width)], [(4,), (4,), ()]
+        functools.partial(pair_kernel, 4), 1, [iterate], [shape(2, block, width)],
+        [(4,), (4,), ()], [(block, width)],
     )
     top = lax.dynamic_slice(pair, (0, (row % 2) * half, 0), (1, half, width))[0]
     near = jnp.concatenate(
@@ -234,7 +290,8 @@
         2,
         [pair, near],
         [shape(rows, block, width), shape(cols, near_rows, block)],
-        [(chunks,)] * 4 + [(cols,), (cols,), (2,)],
+        [(chunks,)] * 4 + [(cols,), (cols,), ()],
+        [(2, block, width), (near_rows, block)],
     )
 
     def summed(parts):
@@ -251,33 +308,20 @@
         3,
         [cross, near_share],
         [shape(cols, cross_rows, block), shape(rows, cols, near_rows, block)],
-        [(cols,), (cols,), (sends,), (rows, cols), (2,)],
+        [(cols,), (cols,), (sends,), (rows, cols), ()],
+        [(cross_rows, block), (near_rows, block)],
     )
     (cross_all,) = call(
         functools.partial(gather_kernel, rows, cols),
         4,
         [summed(got)],
         [shape(rows, cols, cross_rows, block)],
-        [(sends,), (rows, cols), (2,)],
+        [(sends,), (rows, cols), ()],
+        [(cross_rows, block)],
     )
     near_all = near_all.reshape(rows, cols * near_rows, block)
-    cross_all = cross_all.reshape(rows, cols * cross_rows, block)[:, :block]
-    diag = near_all[:, :block]
-    ab = near_all[0:2, block : block + half].reshape(block, block)
-    cd = near_all[2:4, block : block + half].reshape(block, block)
-    ac, bd, cb, da = cross_all[0], cross_all[1], cross_all[2], cross_all[3]
-    gram = jnp.concatenate(
-        [
-            jnp.concatenate([diag[0], ab, ac, da.T], axis=1),
-            jnp.concatenate([ab.T, diag[1], cb.T, bd], axis=1),
-            jnp.concatenate([ac.T, cb, diag[2], cd], axis=1),
-            jnp.concatenate([da, bd.T, cd.T, diag[3]], axis=1),
-        ],
-        axis=0,
-    )
-    gram_rows = lax.dynamic_slice_in_dim(gram, row * block, block, 0)
-    square = jnp.dot(gram_rows, gram, preferred_element_type=jnp.float32)
-    poly = (cubic_coef * gram_rows.astype(jnp.float32) + quintic_coef * square).astype(bf16)
+    cross_all = cross_all.reshape(rows, cols * cross_rows, block)
+    poly = poly_rows(near_all, cross_all, block)
     linear_part = linear_coef * iterate.astype(jnp.float32)
     mixed = linear_part + jnp.dot(
         poly, all_rows.reshape(full, width), preferred_element_type=jnp.float32

time: 783 us -> 347 us (0.44)
  Pallas kernels: 577 us -> 297 us
  other arithmetic: 79 us -> 0.83 us
  local copies, waits for them, and re-layouts: 46.9 us -> 6.55 us
  matrix products: 79.1 us -> 42.5 us
    pallas_call x4, Pallas kernels: 577 us -> 257 us  [call(): pl.pallas_call(kernel, out_shape=outs, in_specs=[ANY] * len(args), out_sp...]
    concatenate x2 -> x0, other arithmetic: 72 us -> none  [the longest x1 67 us: on_device(): jnp.concatenate([jnp.concatenate([diag[0], ab, ac, da.T], axis=1), jnp.co...]
    pallas_call x0 -> x1, Pallas kernels: none -> 40 us  [poly_rows(): pl.pallas_call(poly_kernel, grid=(full // tile,), out_shape=jax.ShapeDtyp...]
    dot_general x1 -> x0, matrix products: 32.5 us -> none  [on_device(): square = jnp.dot(gram_rows, gram, preferred_element_type=jnp.float32)]
    squeeze x5 -> x0, local copies, waits for them, and re-layouts: 20.6 us -> none  [the longest x3 10.7 us: on_device(): ac, bd, cb, da = (cross_all[0], cross_all[1], cross_all[2], cross_all[3])]
    concatenate x1 -> x0, local copies, waits for them, and re-layouts: 9.54 us -> none  [on_device(): jnp.concatenate([diag[0], ab, ac, da.T], axis=1)]
where the time goes in v2:
time: 347 us
  Pallas kernels  297 us (86%)
  matrix products  42.5 us (12%)
  local copies, waits for them, and re-layouts  6.55 us (2%)
    pallas_call x4, Pallas kernels, call(): pl.pallas_call(kernel, out_shape=outs, in_specs=[ANY] * len(args), out_sp...  257 us
    pallas_call x1, Pallas kernels, poly_rows(): pl.pallas_call(poly_kernel, grid=(full // tile,), out_shape=jax.ShapeDtyp...  40 us
    dot_general x1, matrix products, on_device(): jnp.dot(poly, all_rows.reshape(full, width), preferred_element_type=jnp.f...  24 us
    dot_general x3, matrix products, dot_rows(): lax.dot_general(left, right, (((1,), (1,)), ((), ())), preferred_element_...  18.5 us

profile of v2, /device:TPU:0, one launch (start us, length us, event | category | flops | bytes accessed | tf_op | source)
XLA Modules:
  0.0 346.8 jit_solution(13967474185197446235)
XLA Ops:
  0.0 0.0 copy-start.2
  0.0 8.7 %convolution_convert_fusion = bf16[896,896]{1,0:T(8,128)(2,1)S(1)} fusion(bf16[896,2560]{1,0:T(8,128)(2,1)} %x_ref.1), kind=kOutput, calls=%fused_computation.16 | convolution fusion | flops 4111220736 | bytes 6193152 | tf_op jit(solution)/shard_map/dot_general | solution.py:251
  8.8 0.0 copy-done.2
  8.8 7.9 %shard_map.17.pair_ref = bf16[2,896,2560]{2,1,0:T(8,128)(2,1)S(1)} custom-call(bf16[896,2560]{1,0:T(8,128)(2,1)S(1)} %copy-done.2), custom_call_target="tpu_custom_call" | custom-call | tf_op jit(solution)/shard_map/pallas_call | solution.py:237
  16.7 2.6 fusion.14
  19.3 0.2 fusion.8
  19.5 109.0 %shard_map.18 = (bf16[4,896,2560]{2,1,0:T(8,128)(2,1)}, bf16[8,176,896]{2,1,0:T(8,128)(2,1)S(1)}) custom-call(bf16[2,896,2560]{2,1,0:T(8,128)(2,1)S(1)} %shard_map.17.pair_ref, bf16[8,176,896]{2,1,0:T(8,128)(2,1)S(1)} %bitcast.28), custom_call_target="tpu_custom_call" | custom-call | tf_op jit(solution)/shard_map/pallas_call | solution.py:237
  128.5 0.3 convert_reduce_fusion
  128.8 0.1 multiply_convert_fusion.share_ref
  128.9 7.2 %fusion.11 = bf16[896,896]{0,1:T(8,128)(2,1)S(1)} fusion(bf16[896,2560]{1,0:T(8,128)(2,1)S(1)} %copy-done.2, bf16[4,896,2560]{2,1,0:T(8,128)(2,1)} %get-tuple-element.9, s32[]{:T(128)S(6)} %select_n.20), kind=kOutput, calls=%fused_computation.15 | convolution fusion | flops 4111220736 | bytes 10780676 | tf_op jit(solution)/shard_map/dot_general | solution.py:251
  136.1 96.4 %shard_map.19 = (bf16[8,112,896]{2,1,0:T(8,128)(2,1)S(1)}, bf16[4,8,176,896]{3,2,1,0:T(8,128)(2,1)S(1)}) custom-call(bf16[8,112,896]{2,1,0:T(8,128)(2,1)S(1)} %bitcast.30, bf16[176,896]{1,0:T(8,128)(2,1)S(1)} %multiply_convert_fusion.share_ref), custom_call_target="tpu_custom_call" | custom-call | tf_op jit(solution)/shard_map/pallas_call | solution.py:237
  232.5 0.0 copy-start.1
  232.5 3.9 %copy-done.1 = bf16[4,8,176,896]{3,2,1,0:T(8,128)(2,1)} copy-done((bf16[4,8,176,896]{3,2,1,0:T(8,128)(2,1)}, bf16[4,8,176,896]{3,2,1,0:T(8,128)(2,1)S(1)}, u32[]{:S(2)}) %copy-start.1) | copy-done | bytes 10092568
  236.4 0.2 convert_reduce_fusion.1
  236.7 43.5 %shard_map.20 = bf16[4,8,112,896]{3,2,1,0:T(8,128)(2,1)S(1)} custom-call(bf16[112,896]{1,0:T(8,128)(2,1)S(1)} %multiply_convert_fusion.1.share_ref), custom_call_target="tpu_custom_call" | custom-call | tf_op jit(solution)/shard_map/pallas_call | solution.py:237
  280.2 0.0 copy-start
  280.2 2.6 copy-done
  282.9 40.0 %shard_map.21 = bf16[896,3584]{1,0:T(8,128)(2,1)} custom-call(bf16[4,1408,896]{2,1,0:T(8,128)(2,1)} %bitcast.29, bf16[4,896,896]{2,1,0:T(8,128)(2,1)} %bitcast.27), custom_call_target="tpu_custom_call" | custom-call | tf_op jit(solution)/shard_map/pallas_call | solution.py:225
  322.8 24.0 %add_convert_fusion = bf16[896,2560]{1,0:T(8,128)(2,1)} fusion(bf16[896,2560]{1,0:T(8,128)(2,1)S(1)} %copy-done.2, bf16[896,3584]{1,0:T(8,128)(2,1)} %shard_map.21, bf16[3584,2560]{1,0:T(8,128)(2,1)} %bitcast.31), kind=kOutput, calls=%fused_computation | convolution fusion | flops 16450846720 | bytes 33947648 | tf_op jit(solution)/shard_map/dot_general | solution.py:326
  (1 shorter events, 0.0 us)
Async XLA Ops:
  0.0 8.8 %copy-start.2 = (bf16[896,2560]{1,0:T(8,128)(2,1)S(1)}, bf16[896,2560]{1,0:T(8,128)(2,1)}, u32[]{:S(2)}) copy-start(bf16[896,2560]{1,0:T(8,128)(2,1)} %x_ref.1) | copy-start | bytes 13762564
  232.5 3.9 %copy-start.1 = (bf16[4,8,176,896]{3,2,1,0:T(8,128)(2,1)}, bf16[4,8,176,896]{3,2,1,0:T(8,128)(2,1)S(1)}, u32[]{:S(2)}) copy-start(bf16[4,8,176,896]{3,2,1,0:T(8,128)(2,1)S(1)} %get-tuple-element.11) | copy-start | bytes 30277636
  280.2 2.6 copy-start

commit v3 on v2

--- a/solution.py
+++ b/solution.py
@@ -74,12 +74,12 @@
 
 
 def rows_kernel(
-    cols, chunks, pair_ref, part_ref, all_ref, got_ref,
-    y_send, y_recv, f_send, f_recv, s_send, s_recv, local, held, small,
+    cols, chunks, vocab, pair_ref, part_ref, all_ref, near_ref,
+    y_send, y_recv, f_send, f_recv, s_send, s_recv, g_send, g_recv, local, held, parts_held, share_held,
 ):
     row, col = place()
     core = row % 2
-    across, sibling = (flip(row, 2), col), (flip(row, 1), col)
+    across, sibling, side = (flip(row, 2), col), (flip(row, 1), col), (row, flip(col, 1))
     greet([across, sibling] + [(row, (col + k) % cols) for k in range(1, cols)])
     size = pair_ref.shape[1] // chunks
     parts = [pl.ds(j * size, size) for j in range(chunks)]
@@ -90,19 +90,72 @@
         )
         copy.start()
         outgoing.append(copy)
-    scatter = start_scatter(cols, part_ref, got_ref, s_send, s_recv)
-    through_vmem(part_ref.at[col], got_ref.at[0], small, local)
+    scatter = start_scatter(cols, part_ref, parts_held, s_send, s_recv)
+    mine = pltpu.make_async_copy(part_ref.at[col], parts_held.at[0], local)
+    mine.start()
+    mine.wait()
     through_vmem(pair_ref, all_ref.at[pl.ds(row - core, 2)], held, local)
+    for copy in scatter:
+        copy.wait()
+
+    @pl.loop(0, share_held.shape[0], step=16)
+    def _(at):
+        band = pl.ds(pl.multiple_of(at, 16), 16)
+        total = parts_held[0, band, :].astype(jnp.float32)
+        for k in range(1, cols):
+            total = total + parts_held[k, band, :].astype(jnp.float32)
+        share_held[band, :] = (total / vocab).astype(bf16)
+
+    group = cols // 2
+    sent = []
+
+    def push(src, c, peer):
+        copy = remote(src, near_ref.at[row, c], g_send.at[len(sent)], g_recv.at[row % 2, c], peer)
+        copy.start()
+        sent.append(copy)
+
+    def arrived(r, c):
+        slot = near_ref.at[r, c]
+        remote(slot, slot, g_send.at[0], g_recv.at[r % 2, c], sibling).wait_recv()
+
+    def member(m):
+        return ((col // 2 + m) % group) * 2 + col % 2
+
+    for m in range(1, group):
+        push(share_held, col, (row, member(group - m)))
+    push(share_held, col, side)
+    push(share_held, col, sibling)
+    keep = pltpu.make_async_copy(share_held, near_ref.at[row, col], local)
+    keep.start()
+    keep.wait()
     forwards = []
-    for j, part in enumerate(parts):
+
+    def forward(j):
         outgoing[j].wait_recv()
-        there = all_ref.at[flip(row, 2), part]
+        there = all_ref.at[flip(row, 2), parts[j]]
         copy = remote(there, there, f_send.at[j], f_recv.at[j], sibling)
         copy.start()
         forwards.append(copy)
-    for copy in outgoing:
+
+    early = chunks * 3 // 4
+    for j in range(early):
+        forward(j)
+    for m in range(1, group):
+        c = member(m)
+        arrived(row, c)
+        push(near_ref.at[row, c], c, side)
+        push(near_ref.at[row, c], c, sibling)
+    for j in range(early, chunks):
+        forward(j)
+    for m in range(group):
+        c = flip(member(m), 1)
+        arrived(row, c)
+        push(near_ref.at[row, c], c, sibling)
+    for c in range(cols):
+        arrived(flip(row, 1), c)
+    for copy in outgoing + sent:
         copy.wait_send()
-    for copy in scatter + forwards:
+    for copy in forwards:
         copy.wait()
 
 
@@ -168,12 +221,27 @@
     return [(flip(row, 2), col), (flip(row, 1), col)] + [(row, (col + k) % cols) for k in range(1, cols)]
 
 
-def both_kernel(rows, cols, part_ref, share_ref, got_ref, all_ref, s_send, s_recv, g_send, g_recv, local, small, held):
+def both_kernel(rows, cols, part_ref, plane_ref, got_ref, near_ref, s_send, s_recv, g_send, g_recv, local, small):
+    row, col = place()
+    across, sibling = (flip(row, 2), col), (flip(row, 1), col)
     greet(gather_peers(cols))
+    copies = []
+    for c in range(cols):
+        slot = near_ref.at[row, c]
+        copy = remote(slot, slot, g_send.at[0, c], g_recv.at[0, c], across)
+        copy.start()
+        copies.append(copy)
     scatter = start_scatter(cols, part_ref, got_ref, s_send, s_recv)
-    through_vmem(part_ref.at[lax.axis_index("cols")], got_ref.at[0], small, local)
-    gather(rows, cols, share_ref, all_ref, g_send, g_recv, local, held)
-    for copy in scatter:
+    through_vmem(part_ref.at[col], got_ref.at[0], small, local)
+    for c in range(cols):
+        copies[c].wait_recv()
+        slot = near_ref.at[flip(row, 2), c]
+        copy = remote(slot, slot, g_send.at[1, c], g_recv.at[1, c], sibling)
+        copy.start()
+        copies.append(copy)
+    for copy in copies[:cols]:
+        copy.wait_send()
+    for copy in copies[cols:] + scatter:
         copy.wait()
 
 
@@ -233,12 +301,13 @@
     )(near, cross)
 
 
-def call(kernel, ident, args, outs, sems, holds):
+def call(kernel, ident, args, outs, sems, holds, alias={}):
     return pl.pallas_call(
         kernel,
         out_shape=outs,
         in_specs=[ANY] * len(args),
         out_specs=[ANY] * len(outs),
+        input_output_aliases=alias,
         scratch_shapes=[pltpu.SemaphoreType.DMA(shape) for shape in sems]
         + [pltpu.VMEM(shape, bf16) for shape in holds],
         compiler_params=pltpu.CompilerParams(
@@ -285,31 +354,31 @@
     )
     near = chunked(near, cols)
     near_rows = near.shape[1]
-    all_rows, got = call(
-        functools.partial(rows_kernel, cols, chunks),
+    sends = gather_sends(cols)
+    all_rows, near_all = call(
+        functools.partial(rows_kernel, cols, chunks, vocab),
         2,
         [pair, near],
-        [shape(rows, block, width), shape(cols, near_rows, block)],
-        [(chunks,)] * 4 + [(cols,), (cols,), ()],
-        [(2, block, width), (near_rows, block)],
+        [shape(rows, block, width), shape(rows, cols, near_rows, block)],
+        [(chunks,)] * 4 + [(cols,), (cols,), (sends,), (2, cols), ()],
+        [(2, block, width), (cols, near_rows, block), (near_rows, block)],
     )
 
     def summed(parts):
         return (jnp.sum(parts.astype(jnp.float32), axis=0) / vocab).astype(bf16)
 
-    near_share = summed(got)
     other = jnp.where(row < 2, row + 2, rows - 1 - row)
     cross = dot_rows(iterate, lax.dynamic_index_in_dim(all_rows, other, 0, keepdims=False)).astype(bf16)
     cross = chunked(cross, cols)
     cross_rows = cross.shape[1]
-    sends = gather_sends(cols)
     got, near_all = call(
         functools.partial(both_kernel, rows, cols),
         3,
-        [cross, near_share],
+        [cross, near_all],
         [shape(cols, cross_rows, block), shape(rows, cols, near_rows, block)],
-        [(cols,), (cols,), (sends,), (rows, cols), ()],
-        [(cross_rows, block), (near_rows, block)],
+        [(cols,), (cols,), (2, cols), (2, cols), ()],
+        [(cross_rows, block)],
+        {1: 1},
     )
     (cross_all,) = call(
         functools.partial(gather_kernel, rows, cols),

time: 347 us -> 311 us (0.90)
  Pallas kernels: 297 us -> 261 us
    pallas_call x4, Pallas kernels: 257 us -> 221 us  [call(): pl.pallas_call(kernel, out_shape=outs, in_specs=[ANY] * len(args), out_sp...]
where the time goes in v3:
time: 311 us
  Pallas kernels  261 us (84%)
  matrix products  42.4 us (14%)
  local copies, waits for them, and re-layouts  6.52 us (2%)
    pallas_call x4, Pallas kernels, call(): pl.pallas_call(kernel, out_shape=outs, in_specs=[ANY] * len(args), out_sp...  221 us
    pallas_call x1, Pallas kernels, poly_rows(): pl.pallas_call(poly_kernel, grid=(full // tile,), out_shape=jax.ShapeDtyp...  40 us
    dot_general x1, matrix products, on_device(): jnp.dot(poly, all_rows.reshape(full, width), preferred_element_type=jnp.f...  23.9 us
    dot_general x3, matrix products, dot_rows(): lax.dot_general(left, right, (((1,), (1,)), ((), ())), preferred_element_...  18.5 us
    unnamed x6, local copies, waits for them, and re-layouts  6.52 us

profile of v3, /device:TPU:0, one launch (start us, length us, event | category | flops | bytes accessed | tf_op | source)
XLA Modules:
  0.0 310.6 jit_solution(14743327418334030093)
XLA Ops:
  0.0 0.0 copy-start.2
  0.0 8.7 %convolution_convert_fusion = bf16[896,896]{1,0:T(8,128)(2,1)S(1)} fusion(bf16[896,2560]{1,0:T(8,128)(2,1)} %x_ref.1), kind=kOutput, calls=%fused_computation.15 | convolution fusion | flops 4111220736 | bytes 6193152 | tf_op jit(solution)/shard_map/dot_general | solution.py:320
  8.8 0.0 copy-done.2
  8.8 7.9 %shard_map.17.pair_ref = bf16[2,896,2560]{2,1,0:T(8,128)(2,1)S(1)} custom-call(bf16[896,2560]{1,0:T(8,128)(2,1)S(1)} %copy-done.2), custom_call_target="tpu_custom_call" | custom-call | tf_op jit(solution)/shard_map/pallas_call | solution.py:305
  16.7 2.6 fusion.14
  19.3 0.2 fusion.8
  19.5 110.9 %shard_map.18 = (bf16[4,896,2560]{2,1,0:T(8,128)(2,1)}, bf16[4,8,176,896]{3,2,1,0:T(8,128)(2,1)S(1)}) custom-call(bf16[2,896,2560]{2,1,0:T(8,128)(2,1)S(1)} %shard_map.17.pair_ref, bf16[8,176,896]{2,1,0:T(8,128)(2,1)S(1)} %bitcast.29), custom_call_target="tpu_custom_call" | custom-call | tf_op jit(solution)/shard_map/pallas_call | solution.py:305
  130.4 7.2 %fusion.11 = bf16[896,896]{0,1:T(8,128)(2,1)S(1)} fusion(bf16[896,2560]{1,0:T(8,128)(2,1)S(1)} %copy-done.2, bf16[4,896,2560]{2,1,0:T(8,128)(2,1)} %get-tuple-element.9, s32[]{:T(128)S(6)} %select_n.20), kind=kOutput, calls=%fused_computation.14 | convolution fusion | flops 4111220736 | bytes 10780676 | tf_op jit(solution)/shard_map/dot_general | solution.py:320
  137.6 58.9 %shard_map.19 = (bf16[8,112,896]{2,1,0:T(8,128)(2,1)S(1)}, bf16[4,8,176,896]{3,2,1,0:T(8,128)(2,1)S(1)}) custom-call(bf16[8,112,896]{2,1,0:T(8,128)(2,1)S(1)} %bitcast.30, bf16[4,8,176,896]{3,2,1,0:T(8,128)(2,1)S(1)} %get-tuple-element.10.plane_ref), custom_call_target="tpu_custom_call", output_to_operand_aliasing={{1}: (1, {})} | custom-call | tf_op jit(solution)/shard_map/pallas_call | solution.py:305
  196.5 0.0 copy-start
  196.5 3.9 %copy-done = bf16[4,8,176,896]{3,2,1,0:T(8,128)(2,1)} copy-done((bf16[4,8,176,896]{3,2,1,0:T(8,128)(2,1)}, bf16[4,8,176,896]{3,2,1,0:T(8,128)(2,1)S(1)}, u32[]{:S(2)}) %copy-start) | copy-done | bytes 10092568
  200.4 0.2 convert_reduce_fusion
  200.6 43.4 %shard_map.20 = bf16[4,8,112,896]{3,2,1,0:T(8,128)(2,1)S(1)} custom-call(bf16[112,896]{1,0:T(8,128)(2,1)S(1)} %multiply_convert_fusion.share_ref), custom_call_target="tpu_custom_call" | custom-call | tf_op jit(solution)/shard_map/pallas_call | solution.py:305
  244.1 0.0 copy-start.1
  244.1 2.6 copy-done.1
  246.7 40.0 %shard_map.21 = bf16[896,3584]{1,0:T(8,128)(2,1)} custom-call(bf16[4,1408,896]{2,1,0:T(8,128)(2,1)} %bitcast.27, bf16[4,896,896]{2,1,0:T(8,128)(2,1)} %bitcast.28), custom_call_target="tpu_custom_call" | custom-call | tf_op jit(solution)/shard_map/pallas_call | solution.py:293
  286.7 23.9 %add_convert_fusion = bf16[896,2560]{1,0:T(8,128)(2,1)} fusion(bf16[896,2560]{1,0:T(8,128)(2,1)S(1)} %copy-done.2, bf16[896,3584]{1,0:T(8,128)(2,1)} %shard_map.21, bf16[3584,2560]{1,0:T(8,128)(2,1)} %bitcast.31), kind=kOutput, calls=%fused_computation | convolution fusion | flops 16450846720 | bytes 33947648 | tf_op jit(solution)/shard_map/dot_general | solution.py:395
  (1 shorter events, 0.0 us)
Async XLA Ops:
  0.0 8.8 %copy-start.2 = (bf16[896,2560]{1,0:T(8,128)(2,1)S(1)}, bf16[896,2560]{1,0:T(8,128)(2,1)}, u32[]{:S(2)}) copy-start(bf16[896,2560]{1,0:T(8,128)(2,1)} %x_ref.1) | copy-start | bytes 13762564
  196.5 3.9 %copy-start = (bf16[4,8,176,896]{3,2,1,0:T(8,128)(2,1)}, bf16[4,8,176,896]{3,2,1,0:T(8,128)(2,1)S(1)}, u32[]{:S(2)}) copy-start(bf16[4,8,176,896]{3,2,1,0:T(8,128)(2,1)S(1)} %get-tuple-element.11) | copy-start | bytes 30277636
  244.1 2.6 copy-start.1

commit v4 on v3

--- a/solution.py
+++ b/solution.py
@@ -225,23 +225,35 @@
     row, col = place()
     across, sibling = (flip(row, 2), col), (flip(row, 1), col)
     greet(gather_peers(cols))
-    copies = []
-    for c in range(cols):
-        slot = near_ref.at[row, c]
-        copy = remote(slot, slot, g_send.at[0, c], g_recv.at[0, c], across)
-        copy.start()
-        copies.append(copy)
+    side, far, group = (row, flip(col, 1)), flip(row, 2), cols // 2
+    members = [((col // 2 + m) % group) * 2 + col % 2 for m in range(group)]
+    cut = group // 2
+    shared = group - cut
+
+    def push(r, c, send_at, recv_at, peer):
+        slot = near_ref.at[r, c]
+        copy = remote(slot, slot, g_send.at[send_at, c], g_recv.at[recv_at, c], peer)
+        copy.start()
+        return copy
+
+    order = members[cut:] + members[:cut] + [flip(c, 1) for c in members[:cut]]
+    direct = [push(row, c, 0, 0, across) for c in order]
     scatter = start_scatter(cols, part_ref, got_ref, s_send, s_recv)
     through_vmem(part_ref.at[col], got_ref.at[0], small, local)
-    for c in range(cols):
-        copies[c].wait_recv()
-        slot = near_ref.at[flip(row, 2), c]
-        copy = remote(slot, slot, g_send.at[1, c], g_recv.at[1, c], sibling)
-        copy.start()
-        copies.append(copy)
-    for copy in copies[:cols]:
+    passed, forwards = [], []
+    for k, c in enumerate(order):
+        direct[k].wait_recv()
+        if k < shared:
+            passed.append(push(far, c, 2, 0, side))
+        forwards.append(push(far, c, 1, 1, sibling))
+    for c in members[cut:]:
+        c = flip(c, 1)
+        slot = near_ref.at[far, c]
+        remote(slot, slot, g_send.at[0, c], g_recv.at[0, c], side).wait_recv()
+        forwards.append(push(far, c, 1, 1, sibling))
+    for copy in direct + passed:
         copy.wait_send()
-    for copy in copies[cols:] + scatter:
+    for copy in forwards + scatter:
         copy.wait()
 
 
@@ -376,7 +388,7 @@
         3,
         [cross, near_all],
         [shape(cols, cross_rows, block), shape(rows, cols, near_rows, block)],
-        [(cols,), (cols,), (2, cols), (2, cols), ()],
+        [(cols,), (cols,), (3, cols), (2, cols), ()],
         [(cross_rows, block)],
         {1: 1},
     )

time: 311 us -> 298 us (0.958)
  Pallas kernels: 261 us -> 249 us
    pallas_call x4, Pallas kernels: 221 us -> 209 us  [call(): pl.pallas_call(kernel, out_shape=outs, in_specs=[ANY] * len(args), out_sp...]
where the time goes in v4:
time: 298 us
  Pallas kernels  249 us (84%)
  matrix products  42.4 us (14%)
  local copies, waits for them, and re-layouts  6.52 us (2%)
    pallas_call x4, Pallas kernels, call(): pl.pallas_call(kernel, out_shape=outs, in_specs=[ANY] * len(args), out_sp...  209 us
    pallas_call x1, Pallas kernels, poly_rows(): pl.pallas_call(poly_kernel, grid=(full // tile,), out_shape=jax.ShapeDtyp...  40 us
    dot_general x1, matrix products, on_device(): jnp.dot(poly, all_rows.reshape(full, width), preferred_element_type=jnp.f...  23.9 us
    dot_general x3, matrix products, dot_rows(): lax.dot_general(left, right, (((1,), (1,)), ((), ())), preferred_element_...  18.5 us
    unnamed x6, local copies, waits for them, and re-layouts  6.52 us

profile of v4, /device:TPU:0, one launch (start us, length us, event | category | flops | bytes accessed | tf_op | source)
XLA Modules:
  0.0 298.0 jit_solution(16716248918540346184)
XLA Ops:
  0.0 0.0 copy-start.2
  0.0 8.7 %convolution_convert_fusion = bf16[896,896]{1,0:T(8,128)(2,1)S(1)} fusion(bf16[896,2560]{1,0:T(8,128)(2,1)} %x_ref.1), kind=kOutput, calls=%fused_computation.15 | convolution fusion | flops 4111220736 | bytes 6193152 | tf_op jit(solution)/shard_map/dot_general | solution.py:332
  8.8 0.0 copy-done.2
  8.8 7.9 %shard_map.17.pair_ref = bf16[2,896,2560]{2,1,0:T(8,128)(2,1)S(1)} custom-call(bf16[896,2560]{1,0:T(8,128)(2,1)S(1)} %copy-done.2), custom_call_target="tpu_custom_call" | custom-call | tf_op jit(solution)/shard_map/pallas_call | solution.py:317
  16.7 2.6 fusion.14
  19.3 0.2 fusion.8
  19.5 110.9 %shard_map.18 = (bf16[4,896,2560]{2,1,0:T(8,128)(2,1)}, bf16[4,8,176,896]{3,2,1,0:T(8,128)(2,1)S(1)}) custom-call(bf16[2,896,2560]{2,1,0:T(8,128)(2,1)S(1)} %shard_map.17.pair_ref, bf16[8,176,896]{2,1,0:T(8,128)(2,1)S(1)} %bitcast.29), custom_call_target="tpu_custom_call" | custom-call | tf_op jit(solution)/shard_map/pallas_call | solution.py:317
  130.4 7.2 %fusion.11 = bf16[896,896]{0,1:T(8,128)(2,1)S(1)} fusion(bf16[896,2560]{1,0:T(8,128)(2,1)S(1)} %copy-done.2, bf16[4,896,2560]{2,1,0:T(8,128)(2,1)} %get-tuple-element.9, s32[]{:T(128)S(6)} %select_n.20), kind=kOutput, calls=%fused_computation.14 | convolution fusion | flops 4111220736 | bytes 10780676 | tf_op jit(solution)/shard_map/dot_general | solution.py:332
  137.6 46.3 %shard_map.19 = (bf16[8,112,896]{2,1,0:T(8,128)(2,1)S(1)}, bf16[4,8,176,896]{3,2,1,0:T(8,128)(2,1)S(1)}) custom-call(bf16[8,112,896]{2,1,0:T(8,128)(2,1)S(1)} %bitcast.30, bf16[4,8,176,896]{3,2,1,0:T(8,128)(2,1)S(1)} %get-tuple-element.10.plane_ref), custom_call_target="tpu_custom_call", output_to_operand_aliasing={{1}: (1, {})} | custom-call | tf_op jit(solution)/shard_map/pallas_call | solution.py:317
  183.9 0.0 copy-start
  183.9 3.9 %copy-done = bf16[4,8,176,896]{3,2,1,0:T(8,128)(2,1)} copy-done((bf16[4,8,176,896]{3,2,1,0:T(8,128)(2,1)}, bf16[4,8,176,896]{3,2,1,0:T(8,128)(2,1)S(1)}, u32[]{:S(2)}) %copy-start) | copy-done | bytes 10092568
  187.8 0.2 convert_reduce_fusion
  188.1 43.4 %shard_map.20 = bf16[4,8,112,896]{3,2,1,0:T(8,128)(2,1)S(1)} custom-call(bf16[112,896]{1,0:T(8,128)(2,1)S(1)} %multiply_convert_fusion.share_ref), custom_call_target="tpu_custom_call" | custom-call | tf_op jit(solution)/shard_map/pallas_call | solution.py:317
  231.5 0.0 copy-start.1
  231.5 2.6 copy-done.1
  234.1 40.0 %shard_map.21 = bf16[896,3584]{1,0:T(8,128)(2,1)} custom-call(bf16[4,1408,896]{2,1,0:T(8,128)(2,1)} %bitcast.27, bf16[4,896,896]{2,1,0:T(8,128)(2,1)} %bitcast.28), custom_call_target="tpu_custom_call" | custom-call | tf_op jit(solution)/shard_map/pallas_call | solution.py:305
  274.1 23.9 %add_convert_fusion = bf16[896,2560]{1,0:T(8,128)(2,1)} fusion(bf16[896,2560]{1,0:T(8,128)(2,1)S(1)} %copy-done.2, bf16[896,3584]{1,0:T(8,128)(2,1)} %shard_map.21, bf16[3584,2560]{1,0:T(8,128)(2,1)} %bitcast.31), kind=kOutput, calls=%fused_computation | convolution fusion | flops 16450846720 | bytes 33947648 | tf_op jit(solution)/shard_map/dot_general | solution.py:407
  (1 shorter events, 0.0 us)
Async XLA Ops:
  0.0 8.8 %copy-start.2 = (bf16[896,2560]{1,0:T(8,128)(2,1)S(1)}, bf16[896,2560]{1,0:T(8,128)(2,1)}, u32[]{:S(2)}) copy-start(bf16[896,2560]{1,0:T(8,128)(2,1)} %x_ref.1) | copy-start | bytes 13762564
  183.9 3.9 %copy-start = (bf16[4,8,176,896]{3,2,1,0:T(8,128)(2,1)}, bf16[4,8,176,896]{3,2,1,0:T(8,128)(2,1)S(1)}, u32[]{:S(2)}) copy-start(bf16[4,8,176,896]{3,2,1,0:T(8,128)(2,1)S(1)} %get-tuple-element.11) | copy-start | bytes 30277636
  231.5 2.6 copy-start.1
